TPU v7x, 256 devices: a whole 4x4x8 slice. The times are simulated.
256 devices in a mesh: tm: 32 (over z, y), dp: 8 (over x, core).
Axes of the slice: x: 4, y: 4, z: 8, core: 2. Of those that a mesh axis runs over, the one named last changes fastest.
Arguments:
- inputs: bfloat16 [8, 32768, 1024], P('dp', 'tm'), may hold values from -6 to 6
- weights: bfloat16 [1024, 1536], replicated, may hold values from -0.1875 to 0.1875
- out_grad: bfloat16 [8, 32768, 512], P('dp', 'tm'), may hold values from -6 to 6
Outputs:
- input_grad: bfloat16 [8, 32768, 1024], P('dp', 'tm')
- weight_grad: float32 [1024, 1536], P('tm')
All inputs are finite; a program needn't handle non-finite values.
Results may differ from a plain program's by a relative error of at most 0.0075.
Values sent between devices are 32-bit elements; how exact they have to be, the bound alone decides.
No kernel may reach another device: no remote copies, remote signals or barrier semaphores. Data moves between devices by JAX's collectives and lax.ppermute only.
A program may use at most 128 MiB of HBM per device.

v0:
```python
import jax
import jax.numpy as jnp
from jax import lax
from jax.sharding import PartitionSpec as P

H = 4
HD = 128
CH = 256


def carried_in(value, axis, join, neutral, backward):
    count, mine = (lax.axis_size(axis), lax.axis_index(axis))
    pieces = lax.all_gather(value, axis)
    if backward:
        pieces = pieces[::-1]
        mine = count - 1 - mine
    so_far = jnp.full_like(value, 0) + jnp.asarray(neutral, value.dtype)

    def lap(position, so_far):
        longer = join(so_far, pieces[position])
        return jnp.where(position < mine, longer, so_far)

    return lax.fori_loop(0, count - 1, lap, so_far)


def combine(earlier, later):
    return jax.tree.map(jnp.add, earlier, later)


def shards(inputs, weights, out_grad):
    f32 = jnp.float32
    bf16 = jnp.bfloat16
    tok_count = inputs.shape[1]
    width = weights.shape[1] // 3
    block_count = tok_count // CH
    record = inputs[0]
    qkv = jnp.dot(record, weights, preferred_element_type=f32).astype(bf16)
    shape4 = (block_count, CH, H, HD)
    queries = qkv[:, :width].reshape(shape4)
    key_rows = qkv[:, width : 2 * width].reshape(shape4)
    values = qkv[:, 2 * width :].reshape(shape4)
    offset = lax.axis_index("tm") * tok_count
    position = (offset + jnp.arange(tok_count, dtype=jnp.int32)).astype(f32)
    factor = 1.0 / jnp.sqrt(jnp.float32(HD) * (position + 1.0))
    scaled_grad = (out_grad[0].astype(f32) * factor[:, None]).astype(bf16).reshape(shape4)
    tri = (
        lax.broadcasted_iota(jnp.int32, (CH, CH), 0) >= lax.broadcasted_iota(jnp.int32, (CH, CH), 1)
    ).astype(f32)
    kv_group = jnp.einsum("nshd,nshe->nhde", key_rows, values, preferred_element_type=f32)
    qg_group = jnp.einsum("nthd,nthe->nhde", queries, scaled_grad, preferred_element_type=f32)
    kv_device = jnp.sum(kv_group, 0)
    qg_device = jnp.sum(qg_group, 0)
    zeros = jnp.zeros((H, HD, HD), f32)
    state_start = carried_in(kv_device, "tm", combine, zeros, False)
    grad_end = carried_in(qg_device, "tm", combine, zeros, True)
    mix_vg = (
        jnp.einsum("nthe,nshe->nhts", scaled_grad, values, preferred_element_type=f32) * tri
    ).astype(bf16)
    mix_qk = (
        jnp.einsum("nthd,nshd->nhts", queries, key_rows, preferred_element_type=f32) * tri
    ).astype(bf16)
    state_before = (state_start[None] + jnp.cumsum(kv_group, 0) - kv_group).astype(bf16)
    grad_after = (
        grad_end[None] + jnp.flip(jnp.cumsum(jnp.flip(qg_group, 0), 0), 0) - qg_group
    ).astype(bf16)
    grad_q = jnp.einsum(
        "nhts,nshd->nthd", mix_vg, key_rows, preferred_element_type=f32
    ) + jnp.einsum("nthe,nhde->nthd", scaled_grad, state_before, preferred_element_type=f32)
    grad_k = jnp.einsum(
        "nhts,nthd->nshd", mix_vg, queries, preferred_element_type=f32
    ) + jnp.einsum("nshe,nhde->nshd", values, grad_after, preferred_element_type=f32)
    grad_v = jnp.einsum(
        "nhts,nthe->nshe", mix_qk, scaled_grad, preferred_element_type=f32
    ) + jnp.einsum("nshd,nhde->nshe", key_rows, grad_after, preferred_element_type=f32)
    dqkv = jnp.concatenate(
        [
            grad_q.reshape(tok_count, width),
            grad_k.reshape(tok_count, width),
            grad_v.reshape(tok_count, width),
        ],
        axis=1,
    ).astype(bf16)
    record_grad = lax.dot_general(
        dqkv, weights, (((1,), (1,)), ((), ())), preferred_element_type=f32
    ).astype(bf16)
    partial_rows = lax.psum_scatter(
        lax.dot_general(record, dqkv, (((0,), (0,)), ((), ())), preferred_element_type=f32),
        "tm",
        scatter_dimension=0,
        tiled=True,
    )
    proj_grad = lax.psum(partial_rows, "dp")
    return (record_grad[None], proj_grad)


def solution(mesh):
    placed = (P("dp", "tm", None), P(), P("dp", "tm", None))
    return jax.shard_map(
        shards,
        mesh=mesh,
        in_specs=placed,
        out_specs=(P("dp", "tm", None), P("tm", None)),
        check_vma=False,
    )
```

profile of v0, /device:TPU:8, one launch (start us, length us, event | category | flops | bytes accessed | tf_op | source)
XLA Modules:
  0.0 592.0 jit_solution(9342990960004668326)
XLA Ops:
  7.2 2.8 reshape.58
  10.1 2.9 copy.36
  13.0 5.2 convolution_convert_fusion
  20.0 2.2 reshape.55
  22.1 1.9 multiply_convert_fusion.2
  25.1 2.2 fusion.27
  27.4 2.2 reshape.53
  29.5 2.1 reshape.52
  31.7 3.8 fusion.26
  35.7 2.3 rev.11
  38.0 2.5 fusion.28
  40.5 2.3 multiply_convert_fusion.1
  42.9 1.9 fusion.10
  44.7 2.2 fusion.19
  46.9 4.3 fusion.2
  51.1 76.5 %all-gather.7.cloned.1.call-done = f32[128,128,128]{2,1,0:T(8,128)} async-done(((f32[4,128,128]{2,1,0:T(8,128)}), f32[128,128,128]{2,1,0:T(8,128)}) %all-gather.7.cloned.1.call-update) | async-done | bytes 8388624 | tf_op jit(solution)/shard_map/all_gather | solution.py:13
  127.6 7.7 %rev.10 = f32[32,4,128,128]{3,2,1,0:T(8,128)} reverse(f32[32,4,128,128]{3,2,1,0:T(8,128)} %bitcast.53), dimensions={0} | reverse | bytes 16777216 | tf_op jit(solution)/shard_map/rev | solution.py:15
  135.4 54.8 %while.29 = (s32[]{:T(128)}, f32[4,128,128]{2,1,0:T(8,128)}, s32[]{:T(128)}, f32[32,4,128,128]{3,2,1,0:T(8,128)}, s32[]{:T(128)}, /*index=5*/s32[]{:T(128)}) while((s32[]{:T(128)}, f32[4,128,128]{2,1,0:T(8,128)}, s32[]{:T(128)}, f32[32,4,128,128]{3,2,1,0:T(8,128)}, s32[]{:T(128)}, /*index=5*/s32[]{:T(128)}) %tuple.73), condition=%wide.region_6.7_spmd.clone, body=%wide.region_5.6_spmd.clone.sunk | while | flops 196612 | bytes 786525 | solution.py:23
  137.0 1.8 add_select_fusion.5
  138.8 1.8 add_select_fusion.5
  140.6 1.8 add_select_fusion.5
  142.4 1.8 add_select_fusion.5
  144.1 1.8 add_select_fusion.5
  145.9 1.8 add_select_fusion.5
  147.7 1.8 add_select_fusion.5
  149.4 1.8 add_select_fusion.5
  151.2 1.8 add_select_fusion.5
  153.0 1.8 add_select_fusion.5
  154.7 1.8 add_select_fusion.5
  158.3 1.8 add_select_fusion.5
  160.1 1.8 add_select_fusion.5
  161.8 1.8 add_select_fusion.5
  163.6 1.8 add_select_fusion.5
  165.4 1.8 add_select_fusion.5
  167.1 1.8 add_select_fusion.5
  168.9 1.8 add_select_fusion.5
  170.7 1.8 add_select_fusion.5
  172.4 1.8 add_select_fusion.5
  174.2 1.8 add_select_fusion.5
  176.0 1.8 add_select_fusion.5
  179.5 1.8 add_select_fusion.5
  183.1 1.8 add_select_fusion.5
  186.6 1.8 add_select_fusion.5
  188.4 1.8 add_select_fusion.5
  190.2 1.9 subtract_convert_fusion
  192.9 3.2 fusion.5
  196.1 2.3 copy.48
  198.5 27.4 %all-gather.5.cloned.1.call-done = f32[128,128,128]{2,1,0:T(8,128)} async-done(((f32[4,128,128]{2,1,0:T(8,128)}), f32[128,128,128]{2,1,0:T(8,128)}) %all-gather.5.cloned.1.call-update) | async-done | bytes 8388624 | tf_op jit(solution)/shard_map/all_gather | solution.py:13
  225.9 33.0 %while.28 = (s32[]{:T(128)}, f32[4,128,128]{2,1,0:T(8,128)S(1)}, s32[]{:T(128)}, f32[32,4,128,128]{3,2,1,0:T(8,128)}, s32[]{:T(128)}, /*index=5*/s32[]{:T(128)}) while((s32[]{:T(128)}, f32[4,128,128]{2,1,0:T(8,128)S(1)}, s32[]{:T(128)}, f32[32,4,128,128]{3,2,1,0:T(8,128)}, s32[]{:T(128)}, /*index=5*/s32[]{:T(128)}) %tuple.84), condition=%wide.region_2.3_spmd.clone, body=%wide.region_1.0_spmd.clone.sunk | while | flops 196612 | bytes 786525 | solution.py:23
  258.9 1.8 fusion.7
  260.7 3.0 fusion.4
  263.8 2.3 copy.43
  266.1 2.5 bitcast_dynamic-update-slice_fusion.2
  268.6 2.9 fusion.6
  271.5 2.4 copy.53
  273.9 2.6 bitcast_dynamic-update-slice_fusion.1
  276.5 2.4 bitcast_dynamic-update-slice_fusion
  278.9 7.3 %convolution_bitcast_fusion = f32[1024,1536]{0,1:T(8,128)} fusion(bf16[1024,1536]{1,0:T(8,128)(2,1)} %bitcast_dynamic-update-slice_fusion, bf16[1,1024,1024]{2,1,0:T(8,128)(2,1)S(1)} %copy-done.10), kind=kOutput, calls=%fused_computation.2 | convolution fusion | flops 3221225472 | bytes 11534336 | tf_op jit(solution)/shard_map/dot_general | solution.py:87
  286.2 6.6 %copy.59 = f32[1024,1536]{1,0:T(8,128)} copy(f32[1024,1536]{0,1:T(8,128)} %convolution_bitcast_fusion) | data formatting | bytes 12582912
  292.9 222.4 %reduce-scatter.4.cloned.1.call-done = f32[32,1536]{1,0:T(8,128)} async-done(((f32[1024,1536]{1,0:T(8,128)}), f32[32,1536]{1,0:T(8,128)}) %reduce-scatter.4.cloned.1.call-update) | async-done | bytes 196624
  515.3 2.1 copy.60
  517.4 6.5 %convert_bitcast_fusion = bf16[1,1024,1024]{2,1,0:T(8,128)(2,1)} fusion(bf16[1024,1536]{1,0:T(8,128)(2,1)} %bitcast_dynamic-update-slice_fusion, bf16[1024,1536]{1,0:T(8,128)(2,1)S(1)} %copy-done), kind=kOutput, calls=%fused_computation.8 | convolution fusion | flops 3222274048 | bytes 8388608 | tf_op jit(solution)/shard_map/dot_general | solution.py:83
  523.9 59.5 %all-reduce.2.cloned.1.call-done = f32[32,1536]{0,1:T(8,128)} async-done(((f32[32,1536]{0,1:T(8,128)}), f32[32,1536]{0,1:T(8,128)}) %all-reduce.2.cloned.1.call-update) | async-done | bytes 196624 | tf_op jit(solution)/shard_map/psum | solution.py:92
  583.4 2.1 copy.54
  (71 shorter events, 45.1 us)
Async XLA Ops:
  7.2 5.9 copy-start
  7.2 120.5 %all-gather.7.cloned.1.call-start = ((), (), s32[]{:S(2)}) async-start(), calls=%async_computation.3 | async-start | bytes 8650752 | tf_op jit(solution)/shard_map/all_gather | solution.py:13
  22.1 3.0 copy-start.5
  24.0 1.1 copy-start.1
  27.3 198.6 %all-gather.5.cloned.1.call-start = ((), (), s32[]{:S(2)}) async-start(), calls=%async_computation.2 | async-start | bytes 8650752 | tf_op jit(solution)/shard_map/all_gather | solution.py:13
  35.5 479.8 %reduce-scatter.4.cloned.1.call-start = ((), (), s32[]{:S(2)}) async-start(), calls=%async_computation.4 | async-start | bytes 6488064
  38.0 4.8 copy-start.9
  38.0 4.8 copy-start.6
  42.8 1.9 copy-start.3
  190.2 2.7 copy-start.4
  192.1 0.8 copy-start.8
  258.9 1.9 copy-start.2
  266.1 2.5 copy-start.7
  273.9 5.0 copy-start.10
  292.8 290.6 %all-reduce.2.cloned.1.call-start = ((), (), s32[]{:S(2)}) async-start(), calls=%async_computation.1 | async-start | bytes 1572864 | tf_op jit(solution)/shard_map/psum | solution.py:92
Sparse Core Ops, SparseCore 0:
  27.4 100.1 all-gather.6
  130.2 95.6 all-gather.4
  292.9 222.3 reduce-scatter.3
  517.6 65.7 all-reduce.1
where the time goes:
time: 594 us; the launch traced here: 592 us
  waiting for transfers between devices  386 us (65%)
  other arithmetic  95.1 us (16%)
  local copies, waits for them, and re-layouts  51.2 us (9%)
  matrix products  44.8 us (8%)
  between operations  13.9 us (2%)
    unnamed x5, waiting for transfers between devices  222 us
    all_gather x2, waiting for transfers between devices, carried_in(): pieces = lax.all_gather(value, axis)  104 us
    select_n x62, other arithmetic, lap(): return jnp.where(position < mine, longer, so_far)  87.1 us
    psum x1, waiting for transfers between devices, shards(): proj_grad = lax.psum(partial_rows, 'dp')  59.5 us
    unnamed x27, local copies, waits for them, and re-layouts  17.8 us
  transfers between devices with their start and end apart: 4, of which 4 were waited for; matrix products, arithmetic and copies ran while one was open for 17% of the time, Pallas kernels for 0%

commit v1 on v0

--- a/solution.py
+++ b/solution.py
@@ -89,7 +89,7 @@
         scatter_dimension=0,
         tiled=True,
     )
-    proj_grad = lax.psum(partial_rows, "dp")
+    proj_grad = jnp.sum(lax.all_gather(partial_rows, "dp"), axis=0)
     return (record_grad[None], proj_grad)
 
 

time: 594 us -> 555 us (0.934)
  waiting for transfers between devices: 386 us -> 348 us
    unnamed x5 -> x4, waiting for transfers between devices: 222 us -> 0.07 us
    reduce_scatter x0 -> x1, waiting for transfers between devices: none -> 222 us  [shards(): lax.psum_scatter(lax.dot_general(record, dqkv, (((0,), (0,)), ((), ())),...]
    psum x1 -> x0, waiting for transfers between devices: 59.5 us -> none  [shards(): proj_grad = lax.psum(partial_rows, 'dp')]
    all_gather x0 -> x1, waiting for transfers between devices: none -> 21.5 us  [shards(): proj_grad = jnp.sum(lax.all_gather(partial_rows, 'dp'), axis=0)]
    unnamed x27 -> x25, local copies, waits for them, and re-layouts: 17.8 us -> 13.6 us
  transfers between devices with their start and end apart: 4 -> 4, of which waited for: 4 -> 4; matrix products, arithmetic and copies ran while one was open for 17% -> 18% of each run, Pallas kernels for 0% -> 0%
where the time goes in v1:
time: 555 us; the launch traced here: 552 us
  waiting for transfers between devices  348 us (63%)
  other arithmetic  97.3 us (18%)
  local copies, waits for them, and re-layouts  47.1 us (8%)
  matrix products  44.8 us (8%)
  between operations  13.9 us (3%)
    reduce_scatter x1, waiting for transfers between devices, shards(): lax.psum_scatter(lax.dot_general(record, dqkv, (((0,), (0,)), ((), ())),...  222 us
    all_gather x2, waiting for transfers between devices, carried_in(): pieces = lax.all_gather(value, axis)  104 us
    select_n x62, other arithmetic, lap(): return jnp.where(position < mine, longer, so_far)  87.1 us
    all_gather x1, waiting for transfers between devices, shards(): proj_grad = jnp.sum(lax.all_gather(partial_rows, 'dp'), axis=0)  21.5 us
    unnamed x25, local copies, waits for them, and re-layouts  13.6 us
  transfers between devices with their start and end apart: 4, of which 4 were waited for; matrix products, arithmetic and copies ran while one was open for 18% of the time, Pallas kernels for 0%

profile of v1, /device:TPU:8, one launch (start us, length us, event | category | flops | bytes accessed | tf_op | source)
XLA Modules:
  0.0 551.8 jit_solution(15382035294696897876)
XLA Ops:
  7.2 2.8 reshape.58
  10.1 2.9 copy.35
  13.0 5.2 convolution_convert_fusion
  20.0 2.2 reshape.55
  22.1 1.9 multiply_convert_fusion.2
  25.1 2.2 fusion.27
  27.4 2.2 reshape.53
  29.5 2.1 reshape.52
  31.7 3.8 fusion.26
  35.7 2.3 rev.11
  38.0 2.5 fusion.28
  40.5 2.3 multiply_convert_fusion.1
  42.9 1.9 fusion.10
  44.7 2.2 fusion.19
  46.9 4.3 fusion.2
  51.1 76.5 %all-gather.9.cloned.1.call-done = f32[128,128,128]{2,1,0:T(8,128)} async-done(((f32[4,128,128]{2,1,0:T(8,128)}), f32[128,128,128]{2,1,0:T(8,128)}) %all-gather.9.cloned.1.call-update) | async-done | bytes 8388624 | tf_op jit(solution)/shard_map/all_gather | solution.py:13
  127.6 7.7 %rev.10 = f32[32,4,128,128]{3,2,1,0:T(8,128)} reverse(f32[32,4,128,128]{3,2,1,0:T(8,128)} %bitcast.54), dimensions={0} | reverse | bytes 16777216 | tf_op jit(solution)/shard_map/rev | solution.py:15
  135.4 54.8 %while.29 = (s32[]{:T(128)}, f32[4,128,128]{2,1,0:T(8,128)}, s32[]{:T(128)}, f32[32,4,128,128]{3,2,1,0:T(8,128)}, s32[]{:T(128)}, /*index=5*/s32[]{:T(128)}) while((s32[]{:T(128)}, f32[4,128,128]{2,1,0:T(8,128)}, s32[]{:T(128)}, f32[32,4,128,128]{3,2,1,0:T(8,128)}, s32[]{:T(128)}, /*index=5*/s32[]{:T(128)}) %tuple.70), condition=%wide.region_6.7_spmd.clone, body=%wide.region_5.6_spmd.clone.sunk | while | flops 196612 | bytes 786525 | solution.py:23
  137.0 1.8 add_select_fusion.5
  138.8 1.8 add_select_fusion.5
  140.6 1.8 add_select_fusion.5
  142.4 1.8 add_select_fusion.5
  144.1 1.8 add_select_fusion.5
  145.9 1.8 add_select_fusion.5
  147.7 1.8 add_select_fusion.5
  149.4 1.8 add_select_fusion.5
  151.2 1.8 add_select_fusion.5
  153.0 1.8 add_select_fusion.5
  154.7 1.8 add_select_fusion.5
  156.5 1.8 add_select_fusion.5
  158.3 1.8 add_select_fusion.5
  160.1 1.8 add_select_fusion.5
  161.8 1.8 add_select_fusion.5
  163.6 1.8 add_select_fusion.5
  165.4 1.8 add_select_fusion.5
  170.7 1.8 add_select_fusion.5
  172.4 1.8 add_select_fusion.5
  174.2 1.8 add_select_fusion.5
  176.0 1.8 add_select_fusion.5
  177.7 1.8 add_select_fusion.5
  179.5 1.8 add_select_fusion.5
  181.3 1.8 add_select_fusion.5
  183.1 1.8 add_select_fusion.5
  186.6 1.8 add_select_fusion.5
  188.4 1.8 add_select_fusion.5
  190.2 1.9 subtract_convert_fusion
  192.9 3.2 fusion.5
  196.1 2.3 copy.47
  198.5 27.4 %all-gather.7.cloned.1.call-done = f32[128,128,128]{2,1,0:T(8,128)} async-done(((f32[4,128,128]{2,1,0:T(8,128)}), f32[128,128,128]{2,1,0:T(8,128)}) %all-gather.7.cloned.1.call-update) | async-done | bytes 8388624 | tf_op jit(solution)/shard_map/all_gather | solution.py:13
  225.9 33.0 %while.28 = (s32[]{:T(128)}, f32[4,128,128]{2,1,0:T(8,128)S(1)}, s32[]{:T(128)}, f32[32,4,128,128]{3,2,1,0:T(8,128)}, s32[]{:T(128)}, /*index=5*/s32[]{:T(128)}) while((s32[]{:T(128)}, f32[4,128,128]{2,1,0:T(8,128)S(1)}, s32[]{:T(128)}, f32[32,4,128,128]{3,2,1,0:T(8,128)}, s32[]{:T(128)}, /*index=5*/s32[]{:T(128)}) %tuple.81), condition=%wide.region_2.3_spmd.clone, body=%wide.region_1.0_spmd.clone.sunk | while | flops 196612 | bytes 786525 | solution.py:23
  258.9 1.8 fusion.7
  260.7 3.0 fusion.4
  263.8 2.3 copy.42
  266.1 2.5 bitcast_dynamic-update-slice_fusion.2
  268.6 2.9 fusion.6
  271.5 2.4 copy.52
  273.9 2.6 bitcast_dynamic-update-slice_fusion.1
  276.5 2.4 bitcast_dynamic-update-slice_fusion
  278.9 7.3 %convolution_bitcast_fusion = f32[1024,1536]{0,1:T(8,128)} fusion(bf16[1024,1536]{1,0:T(8,128)(2,1)} %bitcast_dynamic-update-slice_fusion, bf16[1,1024,1024]{2,1,0:T(8,128)(2,1)S(1)} %copy-done.10), kind=kOutput, calls=%fused_computation.2 | convolution fusion | flops 3221225472 | bytes 11534336 | tf_op jit(solution)/shard_map/dot_general | solution.py:87
  286.2 6.6 %copy.58 = f32[1024,1536]{1,0:T(8,128)} copy(f32[1024,1536]{0,1:T(8,128)} %convolution_bitcast_fusion) | data formatting | bytes 12582912
  292.9 222.2 %reduce-scatter.4.cloned.1.call-done = f32[32,1536]{1,0:T(8,128)} async-done(((f32[1024,1536]{1,0:T(8,128)}), f32[32,1536]{1,0:T(8,128)}) %reduce-scatter.4.cloned.1.call-update) | async-done | bytes 196624 | tf_op jit(solution)/shard_map/reduce_scatter | solution.py:86
  515.1 6.5 %convert_bitcast_fusion = bf16[1,1024,1024]{2,1,0:T(8,128)(2,1)} fusion(bf16[1024,1536]{1,0:T(8,128)(2,1)} %bitcast_dynamic-update-slice_fusion, bf16[1024,1536]{1,0:T(8,128)(2,1)S(1)} %copy-done), kind=kOutput, calls=%fused_computation.8 | convolution fusion | flops 3222274048 | bytes 8388608 | tf_op jit(solution)/shard_map/dot_general | solution.py:83
  521.6 21.5 %all-gather.11.cloned.1.call-done = f32[256,1536]{1,0:T(8,128)} async-done(((f32[32,1536]{1,0:T(8,128)}), f32[256,1536]{1,0:T(8,128)}) %all-gather.11.cloned.1.call-update) | async-done | bytes 1572880 | tf_op jit(solution)/shard_map/all_gather | solution.py:92
  543.1 2.2 reduce_sum.29
  (70 shorter events, 43.3 us)
Async XLA Ops:
  7.2 5.9 %copy-start = (bf16[1024,1536]{1,0:T(8,128)(2,1)S(1)}, bf16[1024,1536]{1,0:T(8,128)(2,1)}, u32[]{:S(2)}) copy-start(bf16[1024,1536]{1,0:T(8,128)(2,1)} %param.8) | copy-start | bytes 9437188
  7.2 120.5 %all-gather.9.cloned.1.call-start = ((), (), s32[]{:S(2)}) async-start(), calls=%async_computation.2 | async-start | bytes 8650752 | tf_op jit(solution)/shard_map/all_gather | solution.py:13
  22.1 3.0 copy-start.5
  24.0 1.1 copy-start.1
  27.3 198.6 %all-gather.7.cloned.1.call-start = ((), (), s32[]{:S(2)}) async-start(), calls=%async_computation.1 | async-start | bytes 8650752 | tf_op jit(solution)/shard_map/all_gather | solution.py:13
  35.5 479.6 %reduce-scatter.4.cloned.1.call-start = ((), (), s32[]{:S(2)}) async-start(), calls=%async_computation.4 | async-start | bytes 6488064 | tf_op jit(solution)/shard_map/reduce_scatter | solution.py:86
  38.0 4.8 copy-start.9
  38.0 4.8 copy-start.6
  42.8 1.9 copy-start.3
  190.2 2.7 copy-start.4
  192.1 0.8 copy-start.8
  258.9 1.9 copy-start.2
  266.1 2.5 copy-start.7
  273.9 5.0 copy-start.10
  292.8 250.3 %all-gather.11.cloned.1.call-start = ((), (), s32[]{:S(2)}) async-start(), calls=%async_computation.3 | async-start | bytes 1769472 | tf_op jit(solution)/shard_map/all_gather | solution.py:92
Sparse Core Ops, SparseCore 0:
  27.4 100.1 all-gather.8
  130.2 95.6 all-gather.6
  292.9 222.0 reduce-scatter.3
  516.9 26.1 all-gather.10
